TPU v7x, 32 devices: a whole 2x2x4 slice. The times are simulated.
32 devices in a mesh: slab: 8 (over z, y), ang: 4 (over x, core).
Axes of the slice: x: 2, y: 2, z: 4, core: 2. Of those that a mesh axis runs over, the one named last changes fastest.
Arguments:
- conc: bfloat16 [8, 2, 128, 2048], P(None, None, 'slab'), may hold values from 0.049804688 to 1
- spectra: bfloat16 [4, 512, 256], P('ang', 'slab'), may hold values from -4 to 4
- path_slab: int32 [4, 512, 1], P('ang', 'slab'), may hold values from 0 to 7; in each aligned block of 64 rows (0 to 63, 64 to 127, ..., all dimensions but the last counted through in order) at most 16 rows name the same one
- line_offset: int32 [4, 512], P('ang', 'slab'), may hold values from 0 to 31
- profile: float32 [8, 256], replicated, may hold values from 0.01 to 0.3
- beam_absorb: float32 [8], replicated, may hold values from 0.1 to 0.6
- line_absorb: float32 [8, 8], replicated, as said below
Outputs:
- grad_maps: float32 [8, 2, 128, 2048], P(None, None, 'slab', 'ang')
Inputs may be any that keep to these rules, and one draw needn't show every extreme that they name: `path_slab`: among the 64 scan points of one view on one device (aligned blocks), no slab is named more than 16 times, a bound that some block reaches. `line_absorb`: positive coefficients.
All inputs are finite; a program needn't handle non-finite values.
Results may differ from a plain program's by a relative error of at most 0.0003.
Values may be sent and summed in bfloat16 or wider, within the bound.
A program may use at most 64 MiB of HBM per device.

v0:
```python
import jax
import jax.numpy as jnp
from jax import lax
from jax.sharding import PartitionSpec as P

highest = lax.Precision.HIGHEST


def with_halo(block, sides, width):
    for axis, dim in sides:
        count = lax.axis_size(axis)
        forward = [(i, i + 1) for i in range(count - 1)]
        backward = [(target, source) for source, target in forward]
        low = lax.ppermute(
            lax.slice_in_dim(block, block.shape[dim] - width, None, axis=dim), axis, forward
        )
        high = lax.ppermute(lax.slice_in_dim(block, 0, width, axis=dim), axis, backward)
        block = jnp.concatenate([low, block, high], axis=dim)
    return block


def block_prefix(values, forward):
    length = values.shape[-1]
    blocks = length // 128
    inner_row = lax.broadcasted_iota(jnp.int32, (128, 128), 0)
    inner_col = lax.broadcasted_iota(jnp.int32, (128, 128), 1)
    inner_tri = jnp.where(forward, inner_row < inner_col, inner_row > inner_col).astype(jnp.float32)
    outer_row = lax.broadcasted_iota(jnp.int32, (blocks, blocks), 0)
    outer_col = lax.broadcasted_iota(jnp.int32, (blocks, blocks), 1)
    outer_tri = jnp.where(forward, outer_row < outer_col, outer_row > outer_col).astype(jnp.float32)
    shaped = values.reshape(values.shape[:-1] + (blocks, 128))
    within = jnp.einsum("...bi,ij->...bj", shaped, inner_tri, precision=highest)
    carried = jnp.einsum("...a,ab->...b", jnp.sum(shaped, axis=-1), outer_tri, precision=highest)
    return (within + carried[..., None]).reshape(values.shape)


def band_matrix(row_count, band_reach, upward):
    shape = (row_count, row_count + 2 * band_reach)
    out_row = lax.broadcasted_iota(jnp.int32, shape, 0)
    in_row = lax.broadcasted_iota(jnp.int32, shape, 1) - band_reach
    rows_above = (in_row - out_row >= 1) & (in_row - out_row <= band_reach)
    rows_below = (out_row - in_row >= 1) & (out_row - in_row <= band_reach)
    return jnp.where(upward, rows_above, rows_below)


def local(conc, spectra, path_slab, line_offset, profile, beam_absorb, line_absorb):
    element_count, slice_count, row_count, cell_count = conc.shape
    line_count = slice_count * row_count
    view = lax.axis_index("ang")
    forward = view < 2
    upward = view % 2 == 0
    band_reach = row_count // 2
    upper_band = band_matrix(row_count, band_reach, True).astype(jnp.bfloat16)
    lower_band = band_matrix(row_count, band_reach, False).astype(jnp.bfloat16)
    padded = with_halo(conc, (("slab", 2),), band_reach)
    mu_beam = jnp.sum(beam_absorb[:, None, None, None] * conc, axis=0)
    own_band = jnp.where(upward, upper_band, lower_band)
    banded = jnp.einsum("rj,esjc->esrc", own_band, padded, preferred_element_type=jnp.float32)
    line_path = jnp.einsum("ef,fsrc->esrc", line_absorb, banded, precision=highest)
    beam_path = block_prefix(mu_beam, forward) / cell_count
    passing = jnp.exp(-beam_path[None] - line_path)
    fluor = jnp.sum(conc * passing, axis=-1) / cell_count
    fluor_lines = fluor.reshape(element_count, line_count)
    dest = path_slab[0, :, 0]
    offset = line_offset[0]
    ray_count = dest.shape[0]
    slab_count = lax.axis_size("slab")
    capacity = max(2, 2 * ray_count // slab_count)
    slot_count = slab_count * capacity
    dest_hot = (
        dest[:, None] == lax.broadcasted_iota(jnp.int32, (ray_count, slab_count), 1)
    ).astype(jnp.int32)
    ranking = jnp.sum((jnp.cumsum(dest_hot, axis=0) - dest_hot) * dest_hot, axis=1)
    slot = dest * capacity + ranking
    placing = slot[None, :] == lax.broadcasted_iota(jnp.int32, (slot_count, ray_count), 0)
    send_lines = jnp.sum(jnp.where(placing, offset[None, :] + 1, 0), axis=1).reshape(
        slab_count, capacity
    )
    send_rows = jnp.dot(
        placing.astype(jnp.bfloat16), spectra[0], preferred_element_type=jnp.float32
    ).astype(jnp.bfloat16)
    recv_rows, recv_lines = (
        lax.all_to_all(
            send_rows.reshape(slab_count, capacity, -1),
            "slab",
            split_axis=0,
            concat_axis=0,
            tiled=True,
        ),
        lax.all_to_all(send_lines, "slab", split_axis=0, concat_axis=0, tiled=True),
    )
    picking = (
        recv_lines.reshape(slot_count)[:, None] - 1
        == lax.broadcasted_iota(jnp.int32, (slot_count, line_count), 1)
    ).astype(jnp.float32)
    slot_fluor = jnp.dot(picking, fluor_lines.T, precision=highest)
    residual = jnp.dot(slot_fluor, profile, precision=highest) - recv_rows.reshape(
        slot_count, -1
    ).astype(jnp.float32)
    slot_grad = jnp.dot(residual, profile.T, precision=highest)
    line_grad = jnp.dot(slot_grad.T, picking, precision=highest)
    grads_own = line_grad.reshape(element_count, slice_count, row_count)
    weight = -grads_own[..., None] * conc * passing
    back_beam = block_prefix(jnp.sum(weight, axis=0), jnp.logical_not(forward)) / cell_count
    mixed = jnp.einsum("ef,esrc->fsrc", line_absorb, weight, precision=highest)
    padded_mix = with_halo(mixed, (("slab", 2),), band_reach)
    back_band = jnp.where(upward, lower_band, upper_band).astype(jnp.float32)
    back_line = jnp.einsum("rj,fsjc->fsrc", back_band, padded_mix, precision=highest)
    partial_grad = (
        grads_own[..., None] * passing
        + beam_absorb[:, None, None, None] * back_beam[None]
        + back_line
    )
    return lax.psum_scatter(partial_grad, "ang", scatter_dimension=3, tiled=True)


def solution(mesh):
    in_specs = (
        P(None, None, "slab", None),
        P("ang", "slab", None),
        P("ang", "slab", None),
        P("ang", "slab"),
        P(),
        P(),
        P(),
    )
    out_specs = P(None, None, "slab", "ang")
    return jax.shard_map(local, mesh=mesh, in_specs=in_specs, out_specs=out_specs, check_vma=False)
```

profile of v0, /device:TPU:5, one launch (start us, length us, event | category | flops | bytes accessed | tf_op | source)
XLA Modules:
  0.0 152.6 jit_solution(16447887139701638392)
XLA Ops:
  6.5 1.4 fusion.73
  7.9 1.9 %collective-permute-start.1 = (bf16[8,2,8,2048]{3,2,1,0:T(8,128)(2,1)S(1)}, bf16[8,2,8,2048]{3,2,1,0:T(8,128)(2,1)}, u32[]{:S(2)}, u32[]{:S(2)}) collective-permute-start(bf16[8,2,8,2048]{3,2,1,0:T(8,128)(2,1)S(1)} %get-tuple-element.8), channel_id=1, source_target_pairs={{4,0},{8,4},{12,8},{16,12},{20,16},{24,20},{28,24},{5,1},{9,5},{13... | collective-permute-start | bytes 1572872 | tf_op jit(solution)/shard_map/ppermute | solution.py:17
  9.9 4.3 %collective-permute-start = (bf16[8,2,8,2048]{3,2,1,0:T(8,128)(2,1)S(1)}, bf16[8,2,8,2048]{3,2,1,0:T(8,128)(2,1)}, u32[]{:S(2)}, u32[]{:S(2)}) collective-permute-start(bf16[8,2,8,2048]{3,2,1,0:T(8,128)(2,1)S(1)} %get-tuple-element.7), channel_id=1, source_target_pairs={{0,4},{4,8},{8,12},{12,16},{16,20},{20,24},{24,28},{1,5},{5,9},{9,... | collective-permute-start | bytes 1572872 | tf_op jit(solution)/shard_map/ppermute | solution.py:14
  14.6 0.7 all_to_all.9
  15.3 4.8 %all-to-all-start = ((s32[8,1,16]{2,1,0:T(1,128)}), s32[8,1,16]{2,1,0:T(1,128)S(1)}, u32[]{:S(2)}, u32[]{:S(2)}) async-start(s32[8,1,16]{2,1,0:T(1,128)} %bitcast.2), calls=%async_computation | async-start | bytes 8192 | tf_op jit(solution)/shard_map/all_to_all | solution.py:90
  20.1 1.1 fusion.4
  21.4 0.9 convolution_convert_fusion
  22.8 13.1 %all-to-all-done = s32[8,1,16]{2,1,0:T(1,128)S(1)} async-done(((s32[8,1,16]{2,1,0:T(1,128)}), s32[8,1,16]{2,1,0:T(1,128)S(1)}, u32[]{:S(2)}, u32[]{:S(2)}) %all-to-all-start) | async-done | bytes 544 | tf_op jit(solution)/shard_map/all_to_all | solution.py:90
  36.0 4.8 %all-to-all-start.1 = ((bf16[8,16,256]{2,1,0:T(8,128)(2,1)}), bf16[8,16,256]{2,1,0:T(8,128)(2,1)S(1)}, u32[]{:S(2)}, u32[]{:S(2)}) async-start(bf16[8,16,256]{2,1,0:T(8,128)(2,1)} %bitcast.14), calls=%async_computation.1 | async-start | bytes 131072 | tf_op jit(solution)/shard_map/all_to_all | solution.py:83
  40.8 1.6 %convolution_bitcast_fusion = f32[8,2,16,2048]{3,2,1,0:T(8,128)S(1)} fusion(bf16[8,2,8,2048]{3,2,1,0:T(8,128)(2,1)} %collective-permute-done.1, bf16[8,2,16,2048]{3,2,1,0:T(8,128)(2,1)S(1)} %copy-done.1, bf16[8,2,8,2048]{3,2,1,0:T(8,128)(2,1)} %collective-permute-done, s32[32]{0:T(128)S(1)} %iota_add_fusion, pred[]{:T(512)S(6)} %eq.35), kind=kOutput, calls=%fused_computation.6 | convolution fusion | flops 39851520 | bytes 4194433 | tf_op jit(solution)/shard_map/rj,esjc->esrc/dot_general | solution.py:58
  42.5 4.0 %fusion.5 = (f32[8,2,16]{0,2,1:T(8,128)S(1)}, f32[8,2,16,2048]{3,0,2,1:T(8,128)S(1)}) fusion(bf16[8,2,16,2048]{3,2,1,0:T(8,128)(2,1)S(1)} %copy-done.1, f32[8,8]{1,0:T(8,128)S(1)} %copy-done.4, f32[8,2,16,2048]{3,2,1,0:T(8,128)S(1)} %convolution_bitcast_fusion, f32[2,16,2048]{2,1,0:T(8,128)S(1)} %neg.20), kind=kOutput, calls=%fused_computation.12 | convolution fusion | flops 52428544 | bytes 5506304 | tf_op jit(solution)/shard_map/ef,fsrc->esrc/dot_general | solution.py:59
  47.7 2.5 %convolution_bitcast_fusion.1 = f32[8,2,16,2048]{3,0,2,1:T(8,128)S(1)} fusion(f32[8,2,16,2048]{3,0,2,1:T(8,128)S(1)} %get-tuple-element.10, f32[8,2,16]{0,2,1:T(8,128)S(1)} %copy.46, bf16[8,2,16,2048]{3,2,1,0:T(8,128)(2,1)S(1)} %copy-done.1, f32[8,8]{1,0:T(8,128)S(1)} %copy-done.4), kind=kOutput, calls=%fused_computation.7 | convolution fusion | flops 51904512 | bytes 5244160 | tf_op jit(solution)/shard_map/ef,esrc->fsrc/dot_general | solution.py:105
  50.3 1.6 %fusion.72 = (f32[8,2,8,2048]{3,0,2,1:T(8,128)}, f32[8,2,8,2048]{3,0,2,1:T(8,128)}) fusion(f32[8,2,16,2048]{3,0,2,1:T(8,128)S(1)} %convolution_bitcast_fusion.1), kind=kLoop, calls=%fused_computation.94 | loop fusion | bytes 4194304 | tf_op jit(solution)/shard_map/slice | solution.py:15
  51.9 0.4 copy-done.2
  52.3 1.9 %collective-permute-start.3 = (f32[8,2,8,2048]{3,0,2,1:T(8,128)}, f32[8,2,8,2048]{3,0,2,1:T(8,128)}, u32[]{:S(2)}, u32[]{:S(2)}) collective-permute-start(f32[8,2,8,2048]{3,0,2,1:T(8,128)} %get-tuple-element.6), channel_id=1, source_target_pairs={{4,0},{8,4},{12,8},{16,12},{20,16},{24,20},{28,24},{5,1},{9,5},{13... | collective-permute-start | bytes 3145736 | tf_op jit(solution)/shard_map/ppermute | solution.py:17
  54.2 4.4 %collective-permute-start.2 = (f32[8,2,8,2048]{3,0,2,1:T(8,128)}, f32[8,2,8,2048]{3,0,2,1:T(8,128)}, u32[]{:S(2)}, u32[]{:S(2)}) collective-permute-start(f32[8,2,8,2048]{3,0,2,1:T(8,128)} %get-tuple-element.5), channel_id=1, source_target_pairs={{0,4},{4,8},{8,12},{12,16},{16,20},{20,24},{24,28},{1,5},{5,9},{9,... | collective-permute-start | bytes 3145736 | tf_op jit(solution)/shard_map/ppermute | solution.py:14
  58.7 1.3 fusion.14
  60.7 18.3 %collective-permute-done.3 = f32[8,2,8,2048]{3,0,2,1:T(8,128)} collective-permute-done((f32[8,2,8,2048]{3,0,2,1:T(8,128)}, f32[8,2,8,2048]{3,0,2,1:T(8,128)}, u32[]{:S(2)}, u32[]{:S(2)}) %collective-permute-start.3) | collective-permute-done | bytes 1048608 | tf_op jit(solution)/shard_map/ppermute | solution.py:17
  79.0 23.9 %collective-permute-done.2 = f32[8,2,8,2048]{3,0,2,1:T(8,128)} collective-permute-done((f32[8,2,8,2048]{3,0,2,1:T(8,128)}, f32[8,2,8,2048]{3,0,2,1:T(8,128)}, u32[]{:S(2)}, u32[]{:S(2)}) %collective-permute-start.2) | collective-permute-done | bytes 1048608 | tf_op jit(solution)/shard_map/ppermute | solution.py:14
  102.9 2.4 %pad_maximum_fusion = f32[8,2,32,2048]{3,0,2,1:T(8,128)S(1)} fusion(f32[8,2,8,2048]{3,0,2,1:T(8,128)} %collective-permute-done.3, f32[8,2,16,2048]{3,0,2,1:T(8,128)} %copy-done.2, f32[8,2,8,2048]{3,0,2,1:T(8,128)} %collective-permute-done.2), kind=kLoop, calls=%fused_computation | loop fusion | flops 2097152 | bytes 8388608 | tf_op jit(solution)/shard_map/concatenate | solution.py:18
  105.4 4.0 %fusion = f32[8,2,2048,16]{2,3,1,0:T(8,128)S(1)} fusion(f32[8,2,32,2048]{3,0,2,1:T(8,128)S(1)} %pad_maximum_fusion, s32[32]{0:T(128)S(1)} %iota_add_fusion, pred[]{:T(512)S(6)} %eq.35), kind=kOutput, calls=%fused_computation.1 | convolution fusion | flops 201332224 | bytes 6291585 | tf_op jit(solution)/shard_map/rj,fsjc->fsrc/dot_general | solution.py:108
  109.4 2.9 %bitcast_add_fusion = f32[8,2,16,2048]{3,0,2,1:T(8,128)} fusion(f32[8,2,2048,16]{2,3,1,0:T(8,128)S(1)} %fusion, f32[8,2,16,2048]{3,0,2,1:T(8,128)S(1)} %get-tuple-element.10, f32[2,16,2048]{2,1,0:T(8,128)S(1)} %div.21, f32[8,2,16]{0,2,1:T(8,128)S(1)} %copy.44, f32[8]{0:T(128)S(1)} %copy-done.6), kind=kLoop, calls=%fused_computation.19 | loop fusion | flops 2097152 | bytes 6554656 | tf_op jit(solution)/shard_map/add | solution.py:110
  112.3 31.4 %reduce-scatter.2.cloned.1.call-done = f32[8,2,16,512]{3,0,2,1:T(8,128)} async-done(((f32[8,2,16,2048]{3,0,2,1:T(8,128)}), f32[8,2,16,512]{3,0,2,1:T(8,128)}) %reduce-scatter.2.cloned.1.call-update) | async-done | bytes 524304 | tf_op jit(solution)/shard_map/reduce_scatter | solution.py:114
  143.6 2.1 %copy.50 = f32[8,2,16,512]{3,2,1,0:T(8,128)} copy(f32[8,2,16,512]{3,0,2,1:T(8,128)} %reduce-scatter.2.cloned.1.call-done) | data formatting | bytes 1048576 | tf_op jit(solution)/shard_map/reduce_scatter | solution.py:114
  (48 shorter events, 3.1 us)
Async XLA Ops:
  6.5 14.9 %copy-start = (bf16[1,64,256]{2,1,0:T(8,128)(2,1)S(1)}, bf16[1,64,256]{2,1,0:T(8,128)(2,1)}, u32[]{:S(2)}) copy-start(bf16[1,64,256]{2,1,0:T(8,128)(2,1)} %param.8) | copy-start | bytes 98308
  6.5 13.5 %copy-start.1 = (bf16[8,2,16,2048]{3,2,1,0:T(8,128)(2,1)S(1)}, bf16[8,2,16,2048]{3,2,1,0:T(8,128)(2,1)}, u32[]{:S(2)}) copy-start(bf16[8,2,16,2048]{3,2,1,0:T(8,128)(2,1)} %param.7) | copy-start | bytes 3145732
  6.5 7.6 %copy-start.7 = (s32[1,64]{1,0:T(1,128)S(1)}, s32[1,64]{1,0:T(1,128)}, u32[]{:S(2)}) copy-start(s32[1,64]{1,0:T(1,128)} %param.10) | copy-start | bytes 772
  6.5 7.6 %copy-start.5 = (s32[1,64,1]{1,2,0:T(1,128)S(1)}, s32[1,64,1]{1,2,0:T(1,128)}, u32[]{:S(2)}) copy-start(s32[1,64,1]{1,2,0:T(1,128)} %param.9) | copy-start | bytes 772
  6.5 13.5 %copy-start.6 = (f32[8]{0:T(128)S(1)}, f32[8]{0:T(128)}, u32[]{:S(2)}) copy-start(f32[8]{0:T(128)} %param.12) | copy-start | bytes 100
  7.9 32.9 %collective-permute-start.1 = (bf16[8,2,8,2048]{3,2,1,0:T(8,128)(2,1)S(1)}, bf16[8,2,8,2048]{3,2,1,0:T(8,128)(2,1)}, u32[]{:S(2)}, u32[]{:S(2)}) collective-permute-start(bf16[8,2,8,2048]{3,2,1,0:T(8,128)(2,1)S(1)} %get-tuple-element.8), channel_id=1, source_target_pairs={{4,0},{8,4},{12,8},{16,12},{20,16},{24,20},{28,24},{5,1},{9,5},{13... | collective-permute-start | bytes 1572872 | tf_op jit(solution)/shard_map/ppermute | solution.py:17
  9.9 31.0 %collective-permute-start = (bf16[8,2,8,2048]{3,2,1,0:T(8,128)(2,1)S(1)}, bf16[8,2,8,2048]{3,2,1,0:T(8,128)(2,1)}, u32[]{:S(2)}, u32[]{:S(2)}) collective-permute-start(bf16[8,2,8,2048]{3,2,1,0:T(8,128)(2,1)S(1)} %get-tuple-element.7), channel_id=1, source_target_pairs={{0,4},{4,8},{8,12},{12,16},{16,20},{20,24},{24,28},{1,5},{5,9},{9,... | collective-permute-start | bytes 1572872 | tf_op jit(solution)/shard_map/ppermute | solution.py:14
  15.3 20.6 %all-to-all-start = ((s32[8,1,16]{2,1,0:T(1,128)}), s32[8,1,16]{2,1,0:T(1,128)S(1)}, u32[]{:S(2)}, u32[]{:S(2)}) async-start(s32[8,1,16]{2,1,0:T(1,128)} %bitcast.2), calls=%async_computation | async-start | bytes 8192 | tf_op jit(solution)/shard_map/all_to_all | solution.py:90
  36.0 10.8 %all-to-all-start.1 = ((bf16[8,16,256]{2,1,0:T(8,128)(2,1)}), bf16[8,16,256]{2,1,0:T(8,128)(2,1)S(1)}, u32[]{:S(2)}, u32[]{:S(2)}) async-start(bf16[8,16,256]{2,1,0:T(8,128)(2,1)} %bitcast.14), calls=%async_computation.1 | async-start | bytes 131072 | tf_op jit(solution)/shard_map/all_to_all | solution.py:83
  40.7 102.9 %reduce-scatter.2.cloned.1.call-start = ((), (), s32[]{:S(2)}) async-start(), calls=%async_computation.3 | async-start | bytes 2621440 | tf_op jit(solution)/shard_map/reduce_scatter | solution.py:114
  40.8 1.6 %copy-start.4 = (f32[8,8]{1,0:T(8,128)S(1)}, f32[8,8]{1,0:T(8,128)}, u32[]{:S(2)}) copy-start(f32[8,8]{1,0:T(8,128)} %param.13) | copy-start | bytes 772
  42.5 4.3 %copy-start.3 = (f32[8,256]{1,0:T(8,128)S(1)}, f32[8,256]{1,0:T(8,128)}, u32[]{:S(2)}) copy-start(f32[8,256]{1,0:T(8,128)} %param.11) | copy-start | bytes 24580
  50.3 2.0 %copy-start.2 = (f32[8,2,16,2048]{3,0,2,1:T(8,128)}, f32[8,2,16,2048]{3,0,2,1:T(8,128)S(1)}, u32[]{:S(2)}) copy-start(f32[8,2,16,2048]{3,0,2,1:T(8,128)S(1)} %convolution_bitcast_fusion.1) | copy-start | bytes 6291460
  52.3 26.7 %collective-permute-start.3 = (f32[8,2,8,2048]{3,0,2,1:T(8,128)}, f32[8,2,8,2048]{3,0,2,1:T(8,128)}, u32[]{:S(2)}, u32[]{:S(2)}) collective-permute-start(f32[8,2,8,2048]{3,0,2,1:T(8,128)} %get-tuple-element.6), channel_id=1, source_target_pairs={{4,0},{8,4},{12,8},{16,12},{20,16},{24,20},{28,24},{5,1},{9,5},{13... | collective-permute-start | bytes 3145736 | tf_op jit(solution)/shard_map/ppermute | solution.py:17
  54.2 48.7 %collective-permute-start.2 = (f32[8,2,8,2048]{3,0,2,1:T(8,128)}, f32[8,2,8,2048]{3,0,2,1:T(8,128)}, u32[]{:S(2)}, u32[]{:S(2)}) collective-permute-start(f32[8,2,8,2048]{3,0,2,1:T(8,128)} %get-tuple-element.5), channel_id=1, source_target_pairs={{0,4},{4,8},{8,12},{12,16},{16,20},{20,24},{24,28},{1,5},{5,9},{9,... | collective-permute-start | bytes 3145736 | tf_op jit(solution)/shard_map/ppermute | solution.py:14
Sparse Core Ops, SparseCore 0:
  112.4 31.1 reduce-scatter.1
where the time goes:
time: 155 us; the launch traced here: 153 us
  waiting for transfers between devices  86.8 us (56%)
  starting transfers between devices  22.1 us (14%)
  matrix products  15 us (10%)
  between operations  13.7 us (9%)
  other arithmetic  8.46 us (5%)
  local copies, waits for them, and re-layouts  6.71 us (4%)
    reduce_scatter x1, waiting for transfers between devices, local(): lax.psum_scatter(partial_grad, 'ang', scatter_dimension=3, tiled=True)  31.4 us
    ppermute x2, waiting for transfers between devices, with_halo(): lax.ppermute(lax.slice_in_dim(block, block.shape[dim] - width, None, axis...  23.9 us
    ppermute x2, waiting for transfers between devices, with_halo(): lax.ppermute(lax.slice_in_dim(block, 0, width, axis=dim), axis, backward)  18.3 us
    all_to_all x1, waiting for transfers between devices, local(): lax.all_to_all(send_lines, 'slab', split_axis=0, concat_axis=0, tiled=True)  13.1 us
    ppermute x2, starting transfers between devices, with_halo(): lax.ppermute(lax.slice_in_dim(block, block.shape[dim] - width, None, axis...  8.67 us
    all_to_all x1, starting transfers between devices, local(): lax.all_to_all(send_rows.reshape(slab_count, capacity, -1), 'slab', split...  4.76 us
    all_to_all x1, starting transfers between devices, local(): lax.all_to_all(send_lines, 'slab', split_axis=0, concat_axis=0, tiled=True)  4.76 us
    dot_general x1, matrix products, local(): jnp.einsum('rj,fsjc->fsrc', back_band, padded_mix, precision=highest)  4.04 us
  transfers between devices with their start and end apart: 7, of which 4 were waited for; matrix products, arithmetic and copies ran while one was open for 7% of the time, Pallas kernels for 0%

commit v1 on v0

v1 whole, which is shorter than its diff:
```python
import functools

import jax
import jax.numpy as jnp
from jax import lax
from jax.experimental import pallas as pl
from jax.experimental.pallas import tpu as pltpu
from jax.sharding import PartitionSpec as P

f32, bf16, i32 = jnp.float32, jnp.bfloat16, jnp.int32
highest = lax.Precision.HIGHEST
MESH = pl.DeviceIdType.MESH

E, S, R, H = 8, 2, 16, 8
OWN, HALO = E * R, E * H
SIDE = OWN + HALO
LINES = 2 * SIDE


def iota(shape, dim):
    return lax.broadcasted_iota(i32, shape, dim)


def split(x):
    hi = x.astype(bf16)
    return hi, (x - hi.astype(f32)).astype(bf16)


def dot(a, b, precision=None):
    return jnp.dot(a, b, precision=precision, preferred_element_type=f32)


def side_index(index):
    own = index < OWN
    rest = index - OWN
    high = index >= SIDE
    element = jnp.where(own, index // R, (rest % HALO) // H)
    row = jnp.where(own, index % R, jnp.where(high, R, -H) + index % H)
    return element, row


def line_index(index):
    odd = index >= SIDE
    local = jnp.where(odd, index - SIDE, index)
    own = local < OWN
    element = jnp.where(own, local // R, (local - OWN) // H)
    row = jnp.where(own, local % R, jnp.where(odd, R, -H) + local % H)
    return odd, element, row


def kernel(slabs, views, cells, conc_ref, spectra_ref, dest_ref, offset_ref, profile_ref, beam_ref, absorb_ref,
           out_ref, own, low, high, low_out, high_out, fwd_hi, fwd_lo, back_hi, back_lo, tri, gram,
           passing, beams, weights, ray_send, ray_recv, tab, part, column, load_sem,
           halo_send_sem, halo_recv_sem, ray_send_sem, ray_recv_sem, tab_send_sem, tab_recv_sem,
           part_send_sem, part_recv_sem):
    me, block = lax.axis_index("slab"), lax.axis_index("ang")
    width = cells // views
    scale = 1.0 / cells

    loads = []
    for s in range(S):
        copy = pltpu.make_async_copy(
            conc_ref.at[:, s, :, pl.ds(pl.multiple_of(block * width, 128), width)], own.at[s], load_sem.at[s])
        copy.start()
        loads.append(copy)

    barrier = pltpu.get_barrier_semaphore()

    def greet(k, carry):
        pl.semaphore_signal(barrier, inc=1, device_id={"slab": lax.rem(me + k, slabs), "ang": block}, device_id_type=MESH)
        return carry

    lax.fori_loop(1, slabs, greet, 0)
    for k in range(1, views):
        pl.semaphore_signal(barrier, inc=1, device_id={"slab": me, "ang": lax.rem(block + k, views)}, device_id_type=MESH)

    @pl.when(me == 0)
    def _():
        low[...] = jnp.zeros_like(low)

    @pl.when(me == slabs - 1)
    def _():
        high[...] = jnp.zeros_like(high)

    for s in range(S):
        loads[s].wait()
        for i in range(E // 2):
            first = own[s, 2 * i].astype(f32)
            second = own[s, 2 * i + 1].astype(f32)
            low_out[s, i] = jnp.concatenate([first[:H], second[:H]], axis=0).astype(bf16)
            high_out[s, i] = jnp.concatenate([first[H:], second[H:]], axis=0).astype(bf16)

    pl.semaphore_wait(barrier, slabs - 1 + views - 1)

    def halo(s, upward):
        if upward:
            src, dst, target = high_out, low, me + 1
        else:
            src, dst, target = low_out, high, me - 1
        return pltpu.make_async_remote_copy(
            src_ref=src.at[s], dst_ref=dst.at[s],
            send_sem=halo_send_sem.at[int(upward), s], recv_sem=halo_recv_sem.at[int(upward), s],
            device_id={"slab": target, "ang": block}, device_id_type=MESH)

    for s in range(S):
        @pl.when(me < slabs - 1)
        def _():
            halo(s, True).start()

        @pl.when(me > 0)
        def _():
            halo(s, False).start()

    lanes = iota((1, 2 * OWN), 1)
    lane_element, _ = side_index(lanes)
    spread = (iota((E, 2 * OWN), 0) == lane_element).astype(f32)
    profile = profile_ref[...]
    expanded = lax.dot_general(spectra_ref[0].astype(f32), profile, (((1,), (1,)), ((), ())),
                               precision=highest, preferred_element_type=f32)
    rays = expanded.shape[0]
    expanded = dot(expanded, spread, highest)
    offsets = offset_ref[...]
    diagonal = iota((rays, rays), 0) == iota((rays, rays), 1)
    offset_col = jnp.sum(jnp.where(diagonal, offsets.astype(f32), 0.0), axis=1, keepdims=True).astype(i32)
    dest_col = jnp.sum(jnp.where(diagonal, dest_ref[...].astype(f32), 0.0), axis=1, keepdims=True).astype(i32)
    ray_row = dest_col * R + offset_col % R
    odd_view = block % 2
    halo_row = jnp.where(odd_view == 1, R, -H) + lanes % H
    lane_row = jnp.where(lanes < OWN, lanes % R, jnp.where(lanes < SIDE, halo_row, -(1 << 24)))
    row8 = iota((8, rays), 0)
    slice_hot = offsets // R == row8
    pick_sum = jnp.where(slice_hot & (row8 < S), 1.0, 0.0)
    pick_count = jnp.where((offsets // R == row8 - S) & (row8 >= S), 1.0, 0.0)

    def message(target):
        hit = (ray_row - target * R) == lane_row
        return dot(pick_sum, jnp.where(hit, expanded, 0.0), highest) + dot(
            pick_count.astype(bf16), jnp.where(hit, 1.0, 0.0).astype(bf16))

    def ray_copy(k):
        return pltpu.make_async_remote_copy(
            src_ref=ray_send.at[k], dst_ref=ray_recv.at[k], send_sem=ray_send_sem.at[k], recv_sem=ray_recv_sem.at[k],
            device_id={"slab": lax.rem(me + k, slabs), "ang": block}, device_id_type=MESH)

    def send_rays(k, carry):
        ray_send[k] = message(lax.rem(me + k, slabs))
        ray_copy(k).start()
        return carry

    lax.fori_loop(1, slabs, send_rays, 0)
    mine = message(me)

    m_index = iota((LINES, 1), 0)
    odd, m_element, m_row = line_index(m_index)
    k_index = iota((1, 2 * OWN), 1)
    k_element, k_row = side_index(k_index)
    ahead = jnp.where(odd, m_row - k_row, k_row - m_row)
    band = (ahead >= 1) & (ahead <= H)
    rows_hot = (m_element == iota((LINES, E), 1)).astype(bf16)
    cols_hot = spread.astype(bf16)
    absorb = absorb_ref[...]
    for piece, ref in zip(split(absorb), (fwd_hi, fwd_lo)):
        mixed = dot(dot(rows_hot, piece).astype(bf16), cols_hot)
        ref[:LINES] = jnp.where(band, mixed, 0.0).astype(bf16)
    b_row = jnp.zeros((1, 2 * OWN), f32)
    for e in range(E):
        b_row = jnp.where(k_element == e, beam_ref[e], b_row)
    beam_rows = iota((2 * R, 1), 0)
    beam_row = jnp.where(beam_rows < R, beam_rows, jnp.where(beam_rows < R + H, beam_rows - R - H, beam_rows - H))
    beam_mat = jnp.where(beam_row == k_row, b_row, 0.0)
    fwd_hi[LINES:], fwd_lo[LINES:] = split(beam_mat)

    n_index = iota((1, LINES), 1)
    n_odd, n_element, n_row = line_index(n_index)
    o_index = iota((OWN, 1), 0)
    o_element, o_row = o_index // R, o_index % R
    ahead = jnp.where(n_odd, n_row - o_row, o_row - n_row)
    band = (ahead >= 1) & (ahead <= H)
    rows_hot = (o_element == iota((OWN, E), 1)).astype(bf16)
    cols_hot = (iota((E, LINES), 0) == n_element).astype(bf16)
    for piece, ref in zip(split(absorb), (back_hi, back_lo)):
        left = lax.dot_general(rows_hot, piece, (((1,), (1,)), ((), ())), preferred_element_type=f32)
        ref[...] = jnp.where(band, dot(left.astype(bf16), cols_hot), 0.0).astype(bf16)

    tri[...] = jnp.where(iota((width, width), 0) < iota((width, width), 1), 1.0, 0.0).astype(bf16)

    small = lax.dot_general(profile, profile, (((1,), (1,)), ((), ())), precision=highest, preferred_element_type=f32)
    g_rows = iota((2 * OWN, 1), 0)
    g_element, g_row = side_index(g_rows)
    g_hot = (g_element == iota((2 * OWN, E), 1)).astype(f32)
    wide = dot(dot(g_hot, small, highest), spread, highest)
    gram[...] = jnp.where(g_row == k_row, wide, 0.0)


    def gather_rays(k, total):
        ray_copy(k).wait()
        return total + ray_recv[k]

    tab[0] = lax.fori_loop(1, slabs, gather_rays, mine)

    def to_view(ref, k, send, recv):
        return pltpu.make_async_remote_copy(
            src_ref=ref.at[0], dst_ref=ref.at[k], send_sem=send.at[k], recv_sem=recv.at[k],
            device_id={"slab": me, "ang": lax.rem(block + k, views)}, device_id_type=MESH)

    for k in range(1, views):
        to_view(tab, k, tab_send_sem, tab_recv_sem).start()

    lane = iota((1, 128), 1)
    column[...] = jnp.zeros_like(column)
    for s in range(S):
        @pl.when(me > 0)
        def _():
            halo(s, True).wait_recv()

        @pl.when(me < slabs - 1)
        def _():
            halo(s, False).wait_recv()

        maps = jnp.concatenate([own[s], low[s], high[s]], axis=0).reshape(2 * OWN, width)
        paths = dot(fwd_hi[...], maps) + dot(fwd_lo[...], maps)
        passing[s] = jnp.exp(-paths[:LINES])
        mu = paths[LINES:]
        mu_hi, mu_lo = split(mu)
        before = dot(mu_hi, tri[...]) + dot(mu_lo, tri[...])
        total = jnp.sum(mu, axis=1, keepdims=True)
        beams[s, 0] = jnp.exp(-scale * before)
        beams[s, 1] = jnp.exp(-scale * (total - before - mu))

        def put(rows, values, sums):
            merged = column[rows, :]
            for odd_side in range(2):
                for back in range(2):
                    k = 2 * (2 * back + odd_side) + s
                    flux = jnp.sum(values[odd_side][back], axis=1, keepdims=True)
                    merged = jnp.where(lane == k, flux, merged)
                    merged = jnp.where(lane == 8 + k, sums[odd_side], merged)
            column[rows, :] = merged

        for e in range(E):
            amount = own[s, e].astype(f32)
            values = []
            for odd_side in range(2):
                lit = amount * passing[s, odd_side * SIDE + e * R:odd_side * SIDE + (e + 1) * R]
                values.append([lit * beams[s, back, :R] for back in range(2)])
            put(slice(e * R, (e + 1) * R), values, (total[:R], total[:R]))
        for i in range(E // 2):
            values = []
            both = []
            for odd_side, ref in ((0, low), (1, high)):
                start = odd_side * SIDE + OWN + i * 2 * H
                lit = ref[s, i].astype(f32) * passing[s, start:start + 2 * H]
                rows = slice(R + odd_side * H, R + (odd_side + 1) * H)
                values.append([lit * jnp.concatenate([beams[s, back, rows]] * 2, axis=0) for back in range(2)])
                both.append(jnp.concatenate([total[rows]] * 2, axis=0))
            put(slice(OWN + i * 2 * H, OWN + (i + 1) * 2 * H), values, both)

    part[0] = jnp.transpose(column[...])[:16]
    for k in range(1, views):
        to_view(part, k, part_send_sem, part_recv_sem).start()
    for k in range(1, views):
        to_view(tab, k, tab_send_sem, tab_recv_sem).wait()

    row8 = iota((8, 1), 0)
    sums = jnp.zeros((8, 2 * OWN), f32)
    counts = jnp.zeros((8, 2 * OWN), f32)
    owner = [lax.rem(block + views - k, views) for k in range(views)]
    for k in range(views):
        for s in range(S):
            here = row8 == 2 * owner[k] + s
            sums = jnp.where(here, tab[k, s:s + 1, :], sums)
            counts = jnp.where(here, tab[k, S + s:S + s + 1, :], counts)

    for k in range(1, views):
        to_view(part, k, part_send_sem, part_recv_sem).wait()

    ahead_rows = row8 < 4
    blocks, scales = [], []
    for k in range(views):
        offset = jnp.zeros((8, 2 * OWN), f32)
        for j in range(views):
            if j != k:
                counted = (ahead_rows & (owner[j] < owner[k])) | (~ahead_rows & (owner[j] > owner[k]))
                offset = offset + jnp.where(counted, part[j, 8:16, :], 0.0)
        factor = jnp.exp(-scale * offset)
        scales.append(factor)
        blocks.append(part[k, 0:8, :] * factor)
    fluor = (blocks[0] + blocks[1] + blocks[2] + blocks[3]) * scale
    pulled = counts * dot(fluor, gram[...], highest) - sums
    later = jnp.zeros((8, 2 * OWN), f32)
    for k in range(views):
        counted = (ahead_rows & (owner[k] >= block)) | (~ahead_rows & (owner[k] < block))
        later = later + jnp.where(counted, blocks[k], 0.0)
    pad = jnp.zeros((112, 2 * OWN), f32)
    stacked = jnp.concatenate([pulled * scales[0], -pulled * later, pad], axis=0)
    column[...] = jnp.transpose(stacked)

    carry = column[0:R, :]
    for e in range(1, E):
        carry = carry + column[e * R:(e + 1) * R, :]

    for s in range(S):
        beam = [beams[s, 0, :R], beams[s, 1, :R]]
        seen = [jnp.zeros((R, width), f32), jnp.zeros((R, width), f32)]
        for e in range(E):
            amount = own[s, e].astype(f32)
            cols = column[e * R:(e + 1) * R, :]
            direct = None
            for odd_side in range(2):
                start = odd_side * SIDE + e * R
                through = passing[s, start:start + R]
                ahead_pull = cols[:, 2 * odd_side + s:2 * odd_side + s + 1]
                back_pull = cols[:, 4 + 2 * odd_side + s:4 + 2 * odd_side + s + 1]
                term = through * (ahead_pull * beam[0] + back_pull * beam[1])
                lit = amount * through
                seen[0] = seen[0] + lit * ahead_pull
                seen[1] = seen[1] + lit * back_pull
                weights[0, start:start + R], weights[1, start:start + R] = split(amount * term)
                direct = term if direct is None else direct + term
            out_ref[e, s] = direct
        for i in range(E // 2):
            cols = column[OWN + i * 2 * H:OWN + (i + 1) * 2 * H, :]
            for odd_side, ref in ((0, low), (1, high)):
                start = odd_side * SIDE + OWN + i * 2 * H
                rows = slice(R + odd_side * H, R + (odd_side + 1) * H)
                beam_h = [jnp.concatenate([beams[s, back, rows]] * 2, axis=0) for back in range(2)]
                ahead_pull = cols[:, 2 * odd_side + s:2 * odd_side + s + 1]
                back_pull = cols[:, 4 + 2 * odd_side + s:4 + 2 * odd_side + s + 1]
                term = passing[s, start:start + 2 * H] * (ahead_pull * beam_h[0] + back_pull * beam_h[1])
                weights[0, start:start + 2 * H], weights[1, start:start + 2 * H] = split(ref[s, i].astype(f32) * term)
        lines = dot(back_hi[...], weights[0]) + dot(back_lo[...], weights[0]) + dot(back_hi[...], weights[1])
        ahead_sum = beam[0] * seen[0]
        back_sum = beam[1] * seen[1]
        diff_hi, diff_lo = split(ahead_sum - back_sum)
        chosen = (lane >= 8) & (lane < 16) & (lane % 2 == s)
        extra = jnp.sum(jnp.where(chosen, carry, 0.0), axis=1, keepdims=True)
        back_beam = scale * (dot(diff_hi, tri[...]) + dot(diff_lo, tri[...]) + ahead_sum + extra)
        for e in range(E):
            out_ref[e, s] = out_ref[e, s] + beam_ref[e] * back_beam - lines[e * R:(e + 1) * R]

    for s in range(S):
        @pl.when(me < slabs - 1)
        def _():
            halo(s, True).wait_send()

        @pl.when(me > 0)
        def _():
            halo(s, False).wait_send()


def local(slabs, views, conc, spectra, path_slab, line_offset, profile, beam_absorb, line_absorb):
    cells = conc.shape[-1]
    width = cells // views
    vmem, smem = pl.BlockSpec(memory_space=pltpu.VMEM), pl.BlockSpec(memory_space=pltpu.SMEM)
    dma = pltpu.SemaphoreType.DMA
    return pl.pallas_call(
        functools.partial(kernel, slabs, views, cells),
        out_shape=jax.ShapeDtypeStruct((E, S, R, width), f32),
        in_specs=[pl.BlockSpec(memory_space=pl.ANY), vmem, vmem, vmem, vmem, smem, vmem],
        out_specs=vmem,
        scratch_shapes=[
            pltpu.VMEM((S, E, R, width), bf16),
            pltpu.VMEM((S, E // 2, 2 * H, width), bf16),
            pltpu.VMEM((S, E // 2, 2 * H, width), bf16),
            pltpu.VMEM((S, E // 2, 2 * H, width), bf16),
            pltpu.VMEM((S, E // 2, 2 * H, width), bf16),
            pltpu.VMEM((LINES + 2 * R, 2 * OWN), bf16),
            pltpu.VMEM((LINES + 2 * R, 2 * OWN), bf16),
            pltpu.VMEM((OWN, LINES), bf16),
            pltpu.VMEM((OWN, LINES), bf16),
            pltpu.VMEM((width, width), bf16),
            pltpu.VMEM((2 * OWN, 2 * OWN), f32),
            pltpu.VMEM((S, LINES, width), f32),
            pltpu.VMEM((S, 2, 2 * R, width), f32),
            pltpu.VMEM((2, LINES, width), bf16),
            pltpu.VMEM((slabs, 8, 2 * OWN), f32),
            pltpu.VMEM((slabs, 8, 2 * OWN), f32),
            pltpu.VMEM((views, 8, 2 * OWN), f32),
            pltpu.VMEM((views, 16, 2 * OWN), f32),
            pltpu.VMEM((2 * OWN, 128), f32),
            dma((S,)),
            dma((2, S)),
            dma((2, S)),
            dma((slabs,)),
            dma((slabs,)),
            dma((views,)),
            dma((views,)),
            dma((views,)),
            dma((views,)),
        ],
        compiler_params=pltpu.CompilerParams(
            collective_id=0, has_side_effects=True, vmem_limit_bytes=40 * 1024 * 1024),
    )(conc, spectra, path_slab.reshape(1, -1), line_offset, profile, beam_absorb, line_absorb)


def solution(mesh):
    slabs, views = mesh.shape["slab"], mesh.shape["ang"]
    in_specs = (
        P(None, None, "slab", None),
        P("ang", "slab", None),
        P("ang", "slab", None),
        P("ang", "slab"),
        P(),
        P(),
        P(),
    )
    out_specs = P(None, None, "slab", "ang")
    return jax.shard_map(functools.partial(local, slabs, views), mesh=mesh, in_specs=in_specs, out_specs=out_specs,
                         check_vma=False)
```

time: 155 us -> 25.5 us (0.16)
  the two profiles are of different devices: /device:TPU:5 before, /device:TPU:0 now
where the time goes in v1:
time: 25.5 us; the launch traced here: 25.2 us
  Pallas kernels  20.3 us (80%)
  local copies, waits for them, and re-layouts  4.84 us (19%)
    pallas_call x1, Pallas kernels, local(): pl.pallas_call(functools.partial(kernel, slabs, views, cells), out_shape=...  20.3 us
    unnamed x15, local copies, waits for them, and re-layouts  4.84 us

profile of v1, /device:TPU:0, one launch (start us, length us, event | category | flops | bytes accessed | tf_op | source)
XLA Modules:
  0.0 25.2 jit_solution(5312239064698589462)
XLA Ops:
  0.0 0.0 copy-start.6
  0.0 0.0 copy-start.5
  0.0 0.0 copy-start.4
  0.0 0.6 %copy-done.6 = f32[8]{0:T(128)S(1)} copy-done((f32[8]{0:T(128)S(1)}, f32[8]{0:T(128)}, u32[]{:S(2)}) %copy-start.6) | copy-done | bytes 56
  0.7 0.0 copy-done.5
  0.7 0.0 copy-done.4
  0.7 0.0 copy-start
  0.7 1.2 %copy-done = bf16[8,2,16,2048]{3,2,1,0:T(8,128)(2,1)S(1)} copy-done((bf16[8,2,16,2048]{3,2,1,0:T(8,128)(2,1)S(1)}, bf16[8,2,16,2048]{3,2,1,0:T(8,128)(2,1)}, u32[]{:S(2)}) %copy-start) | copy-done | bytes 1048600
  1.9 0.0 copy-start.1
  1.9 0.8 %copy-done.1 = bf16[1,64,256]{2,1,0:T(8,128)(2,1)S(1)} copy-done((bf16[1,64,256]{2,1,0:T(8,128)(2,1)S(1)}, bf16[1,64,256]{2,1,0:T(8,128)(2,1)}, u32[]{:S(2)}) %copy-start.1) | copy-done | bytes 32792
  2.7 0.0 copy-start.2
  2.7 0.7 %copy-done.2 = f32[8,256]{1,0:T(8,128)S(1)} copy-done((f32[8,256]{1,0:T(8,128)S(1)}, f32[8,256]{1,0:T(8,128)}, u32[]{:S(2)}) %copy-start.2) | copy-done | bytes 8216
  3.4 0.0 copy-start.3
  3.4 0.7 %copy-done.3 = f32[8,8]{1,0:T(8,128)S(1)} copy-done((f32[8,8]{1,0:T(8,128)S(1)}, f32[8,8]{1,0:T(8,128)}, u32[]{:S(2)}) %copy-start.3) | copy-done | bytes 280
  4.1 20.3 %shard_map.73 = f32[8,2,16,512]{3,2,1,0:T(8,128)S(1)} custom-call(bf16[8,2,16,2048]{3,2,1,0:T(8,128)(2,1)S(1)} %copy-done, bf16[1,64,256]{2,1,0:T(8,128)(2,1)S(1)} %copy-done.1, s32[1,64]{1,0:T(1,128)S(1)} %bitcast.1, s32[1,64]{1,0:T(1,128)S(1)} %copy-done.5, f32[8,256]{1,0:T(8,128)S(1)} %copy-done.2, f32[8]{0:T(128)S(1)} %copy-done.6, f32[8,8]{1,0:T(8,128)S(1)} %copy-done.3), custom_call_target="tpu_custom_call" | custom-call | tf_op jit(solution)/shard_map/pallas_call | solution.py:356
  24.4 0.8 %copy.9 = f32[8,2,16,512]{3,2,1,0:T(8,128)} copy(f32[8,2,16,512]{3,2,1,0:T(8,128)S(1)} %shard_map.73) | data formatting | bytes 1048576
Async XLA Ops:
  0.0 0.7 %copy-start.6 = (f32[8]{0:T(128)S(1)}, f32[8]{0:T(128)}, u32[]{:S(2)}) copy-start(f32[8]{0:T(128)} %beam_ref.1) | copy-start | bytes 100
  0.0 0.7 %copy-start.5 = (s32[1,64]{1,0:T(1,128)S(1)}, s32[1,64]{1,0:T(1,128)}, u32[]{:S(2)}) copy-start(s32[1,64]{1,0:T(1,128)} %offset_ref.1) | copy-start | bytes 772
  0.0 0.7 %copy-start.4 = (s32[1,64,1]{1,2,0:T(1,128)S(1)}, s32[1,64,1]{1,2,0:T(1,128)}, u32[]{:S(2)}) copy-start(s32[1,64,1]{1,2,0:T(1,128)} %param.9) | copy-start | bytes 772
  0.7 1.2 %copy-start = (bf16[8,2,16,2048]{3,2,1,0:T(8,128)(2,1)S(1)}, bf16[8,2,16,2048]{3,2,1,0:T(8,128)(2,1)}, u32[]{:S(2)}) copy-start(bf16[8,2,16,2048]{3,2,1,0:T(8,128)(2,1)} %conc_ref.1) | copy-start | bytes 3145732
  1.9 0.8 %copy-start.1 = (bf16[1,64,256]{2,1,0:T(8,128)(2,1)S(1)}, bf16[1,64,256]{2,1,0:T(8,128)(2,1)}, u32[]{:S(2)}) copy-start(bf16[1,64,256]{2,1,0:T(8,128)(2,1)} %spectra_ref.1) | copy-start | bytes 98308
  2.7 0.7 %copy-start.2 = (f32[8,256]{1,0:T(8,128)S(1)}, f32[8,256]{1,0:T(8,128)}, u32[]{:S(2)}) copy-start(f32[8,256]{1,0:T(8,128)} %profile_ref.1) | copy-start | bytes 24580
  3.4 0.7 %copy-start.3 = (f32[8,8]{1,0:T(8,128)S(1)}, f32[8,8]{1,0:T(8,128)}, u32[]{:S(2)}) copy-start(f32[8,8]{1,0:T(8,128)} %absorb_ref.1) | copy-start | bytes 772

commit v2 on v1

--- a/solution.py
+++ b/solution.py
@@ -34,8 +34,8 @@
     own = index < OWN
     rest = index - OWN
     high = index >= SIDE
-    element = jnp.where(own, index // R, (rest % HALO) // H)
-    row = jnp.where(own, index % R, jnp.where(high, R, -H) + index % H)
+    element = jnp.where(own, index >> 4, (rest & (HALO - 1)) >> 3)
+    row = jnp.where(own, index & (R - 1), jnp.where(high, R, -H) + (index & (H - 1)))
     return element, row
 
 
@@ -43,16 +43,18 @@
     odd = index >= SIDE
     local = jnp.where(odd, index - SIDE, index)
     own = local < OWN
-    element = jnp.where(own, local // R, (local - OWN) // H)
-    row = jnp.where(own, local % R, jnp.where(odd, R, -H) + local % H)
+    element = jnp.where(own, local >> 4, (local - OWN) >> 3)
+    row = jnp.where(own, local & (R - 1), jnp.where(odd, R, -H) + (local & (H - 1)))
     return odd, element, row
 
 
-def kernel(slabs, views, cells, conc_ref, spectra_ref, dest_ref, offset_ref, profile_ref, beam_ref, absorb_ref,
-           out_ref, own, low, high, low_out, high_out, fwd_hi, fwd_lo, back_hi, back_lo, tri, gram,
-           passing, beams, weights, ray_send, ray_recv, tab, part, column, load_sem,
-           halo_send_sem, halo_recv_sem, ray_send_sem, ray_recv_sem, tab_send_sem, tab_recv_sem,
-           part_send_sem, part_recv_sem):
+def kernel(slabs, views, cells, conc_ref, *refs):
+    small_in, out_ref, small_refs, rest = refs[:6], refs[6], refs[7:13], refs[13:]
+    spectra_ref, dest_ref, offset_ref, profile_ref, beam_ref, absorb_ref = small_refs
+    (own, low, high, low_out, high_out, fwd_hi, fwd_lo, back_hi, back_lo, tri, gram_hi, gram_lo,
+     passing, beams, weights, ray_send, ray_recv, tab, part, column, load_sem, small_sem,
+     halo_send_sem, halo_recv_sem, ray_send_sem, ray_recv_sem, tab_send_sem, tab_recv_sem,
+     part_send_sem, part_recv_sem) = rest
     me, block = lax.axis_index("slab"), lax.axis_index("ang")
     width = cells // views
     scale = 1.0 / cells
@@ -63,6 +65,11 @@
             conc_ref.at[:, s, :, pl.ds(pl.multiple_of(block * width, 128), width)], own.at[s], load_sem.at[s])
         copy.start()
         loads.append(copy)
+    small_loads = []
+    for i in range(6):
+        copy = pltpu.make_async_copy(small_in[i], small_refs[i], small_sem.at[i])
+        copy.start()
+        small_loads.append(copy)
 
     barrier = pltpu.get_barrier_semaphore()
 
@@ -111,31 +118,34 @@
         def _():
             halo(s, False).start()
 
+    for copy in small_loads:
+        copy.wait()
     lanes = iota((1, 2 * OWN), 1)
     lane_element, _ = side_index(lanes)
     spread = (iota((E, 2 * OWN), 0) == lane_element).astype(f32)
     profile = profile_ref[...]
-    expanded = lax.dot_general(spectra_ref[0].astype(f32), profile, (((1,), (1,)), ((), ())),
-                               precision=highest, preferred_element_type=f32)
-    rays = expanded.shape[0]
-    expanded = dot(expanded, spread, highest)
+    flat = (((1,), (1,)), ((), ()))
+    lines_of = sum(lax.dot_general(spectra_ref[0], piece, flat, preferred_element_type=f32) for piece in split(profile))
+    rays = lines_of.shape[0]
+    expanded = [dot(piece, spread.astype(bf16)) for piece in split(lines_of)]
     offsets = offset_ref[...]
     diagonal = iota((rays, rays), 0) == iota((rays, rays), 1)
-    offset_col = jnp.sum(jnp.where(diagonal, offsets.astype(f32), 0.0), axis=1, keepdims=True).astype(i32)
-    dest_col = jnp.sum(jnp.where(diagonal, dest_ref[...].astype(f32), 0.0), axis=1, keepdims=True).astype(i32)
-    ray_row = dest_col * R + offset_col % R
+    ray_row = (dest_ref[...] << 4) + (offsets & (R - 1))
+    ray_row = jnp.sum(jnp.where(diagonal, ray_row, 0).astype(f32), axis=1, keepdims=True).astype(i32)
     odd_view = block % 2
-    halo_row = jnp.where(odd_view == 1, R, -H) + lanes % H
-    lane_row = jnp.where(lanes < OWN, lanes % R, jnp.where(lanes < SIDE, halo_row, -(1 << 24)))
+    halo_row = jnp.where(odd_view == 1, R, -H) + (lanes & (H - 1))
+    lane_row = jnp.where(lanes < OWN, lanes & (R - 1), jnp.where(lanes < SIDE, halo_row, -(1 << 24)))
+    ray_gap = ray_row - lane_row
     row8 = iota((8, rays), 0)
-    slice_hot = offsets // R == row8
-    pick_sum = jnp.where(slice_hot & (row8 < S), 1.0, 0.0)
-    pick_count = jnp.where((offsets // R == row8 - S) & (row8 >= S), 1.0, 0.0)
+    ray_slice = offsets >> 4
+    pick_sum = jnp.where(ray_slice == row8, 1.0, 0.0)
+    pick_count = jnp.where(ray_slice == row8 - S, 1.0, 0.0)
+    pick = jnp.concatenate([pick_sum, pick_sum, pick_count, jnp.zeros_like(pick_sum)], axis=1).astype(bf16)
 
     def message(target):
-        hit = (ray_row - target * R) == lane_row
-        return dot(pick_sum, jnp.where(hit, expanded, 0.0), highest) + dot(
-            pick_count.astype(bf16), jnp.where(hit, 1.0, 0.0).astype(bf16))
+        hit = ray_gap == target * R
+        picked = [jnp.where(hit, x, 0.0) for x in (*expanded, 1.0)]
+        return dot(pick, jnp.concatenate(picked + [jnp.zeros_like(picked[0])], axis=0).astype(bf16))
 
     def ray_copy(k):
         return pltpu.make_async_remote_copy(
@@ -173,7 +183,7 @@
     n_index = iota((1, LINES), 1)
     n_odd, n_element, n_row = line_index(n_index)
     o_index = iota((OWN, 1), 0)
-    o_element, o_row = o_index // R, o_index % R
+    o_element, o_row = o_index >> 4, o_index & (R - 1)
     ahead = jnp.where(n_odd, n_row - o_row, o_row - n_row)
     band = (ahead >= 1) & (ahead <= H)
     rows_hot = (o_element == iota((OWN, E), 1)).astype(bf16)
@@ -184,27 +194,13 @@
 
     tri[...] = jnp.where(iota((width, width), 0) < iota((width, width), 1), 1.0, 0.0).astype(bf16)
 
-    small = lax.dot_general(profile, profile, (((1,), (1,)), ((), ())), precision=highest, preferred_element_type=f32)
+    small = lax.dot_general(profile, profile, flat, precision=highest, preferred_element_type=f32)
     g_rows = iota((2 * OWN, 1), 0)
     g_element, g_row = side_index(g_rows)
-    g_hot = (g_element == iota((2 * OWN, E), 1)).astype(f32)
-    wide = dot(dot(g_hot, small, highest), spread, highest)
-    gram[...] = jnp.where(g_row == k_row, wide, 0.0)
-
-
-    def gather_rays(k, total):
-        ray_copy(k).wait()
-        return total + ray_recv[k]
-
-    tab[0] = lax.fori_loop(1, slabs, gather_rays, mine)
-
-    def to_view(ref, k, send, recv):
-        return pltpu.make_async_remote_copy(
-            src_ref=ref.at[0], dst_ref=ref.at[k], send_sem=send.at[k], recv_sem=recv.at[k],
-            device_id={"slab": me, "ang": lax.rem(block + k, views)}, device_id_type=MESH)
-
-    for k in range(1, views):
-        to_view(tab, k, tab_send_sem, tab_recv_sem).start()
+    g_hot = (g_element == iota((2 * OWN, E), 1)).astype(bf16)
+    for piece, ref in zip(split(small), (gram_hi, gram_lo)):
+        wide = dot(dot(g_hot, piece).astype(bf16), spread.astype(bf16))
+        ref[...] = jnp.where(g_row == k_row, wide, 0.0).astype(bf16)
 
     lane = iota((1, 128), 1)
     column[...] = jnp.zeros_like(column)
@@ -255,9 +251,23 @@
                 both.append(jnp.concatenate([total[rows]] * 2, axis=0))
             put(slice(OWN + i * 2 * H, OWN + (i + 1) * 2 * H), values, both)
 
+
+    def gather_rays(k, total):
+        ray_copy(k).wait()
+        return total + ray_recv[k]
+
+    def to_view(ref, k, send, recv):
+        return pltpu.make_async_remote_copy(
+            src_ref=ref.at[0], dst_ref=ref.at[k], send_sem=send.at[k], recv_sem=recv.at[k],
+            device_id={"slab": me, "ang": lax.rem(block + k, views)}, device_id_type=MESH)
+
     part[0] = jnp.transpose(column[...])[:16]
     for k in range(1, views):
         to_view(part, k, part_send_sem, part_recv_sem).start()
+    tab[0] = lax.fori_loop(1, slabs, gather_rays, mine)
+    for k in range(1, views):
+        to_view(tab, k, tab_send_sem, tab_recv_sem).start()
+
     for k in range(1, views):
         to_view(tab, k, tab_send_sem, tab_recv_sem).wait()
 
@@ -286,7 +296,9 @@
         scales.append(factor)
         blocks.append(part[k, 0:8, :] * factor)
     fluor = (blocks[0] + blocks[1] + blocks[2] + blocks[3]) * scale
-    pulled = counts * dot(fluor, gram[...], highest) - sums
+    fluor_hi, fluor_lo = split(fluor)
+    mixed = dot(fluor_hi, gram_hi[...]) + dot(fluor_lo, gram_hi[...]) + dot(fluor_hi, gram_lo[...])
+    pulled = counts * mixed - sums
     later = jnp.zeros((8, 2 * OWN), f32)
     for k in range(views):
         counted = (ahead_rows & (owner[k] >= block)) | (~ahead_rows & (owner[k] < block))
@@ -351,14 +363,16 @@
 def local(slabs, views, conc, spectra, path_slab, line_offset, profile, beam_absorb, line_absorb):
     cells = conc.shape[-1]
     width = cells // views
-    vmem, smem = pl.BlockSpec(memory_space=pltpu.VMEM), pl.BlockSpec(memory_space=pltpu.SMEM)
+    inputs = (conc, spectra, path_slab.reshape(1, -1), line_offset, profile, beam_absorb, line_absorb)
     dma = pltpu.SemaphoreType.DMA
     return pl.pallas_call(
         functools.partial(kernel, slabs, views, cells),
         out_shape=jax.ShapeDtypeStruct((E, S, R, width), f32),
-        in_specs=[pl.BlockSpec(memory_space=pl.ANY), vmem, vmem, vmem, vmem, smem, vmem],
-        out_specs=vmem,
+        in_specs=[pl.BlockSpec(memory_space=pltpu.HBM)] * len(inputs),
+        out_specs=pl.BlockSpec(memory_space=pltpu.VMEM),
         scratch_shapes=[
+            pltpu.SMEM(x.shape, x.dtype) if x is beam_absorb else pltpu.VMEM(x.shape, x.dtype) for x in inputs[1:]
+        ] + [
             pltpu.VMEM((S, E, R, width), bf16),
             pltpu.VMEM((S, E // 2, 2 * H, width), bf16),
             pltpu.VMEM((S, E // 2, 2 * H, width), bf16),
@@ -369,7 +383,8 @@
             pltpu.VMEM((OWN, LINES), bf16),
             pltpu.VMEM((OWN, LINES), bf16),
             pltpu.VMEM((width, width), bf16),
-            pltpu.VMEM((2 * OWN, 2 * OWN), f32),
+            pltpu.VMEM((2 * OWN, 2 * OWN), bf16),
+            pltpu.VMEM((2 * OWN, 2 * OWN), bf16),
             pltpu.VMEM((S, LINES, width), f32),
             pltpu.VMEM((S, 2, 2 * R, width), f32),
             pltpu.VMEM((2, LINES, width), bf16),
@@ -379,6 +394,7 @@
             pltpu.VMEM((views, 16, 2 * OWN), f32),
             pltpu.VMEM((2 * OWN, 128), f32),
             dma((S,)),
+            dma((len(inputs) - 1,)),
             dma((2, S)),
             dma((2, S)),
             dma((slabs,)),
@@ -389,8 +405,8 @@
             dma((views,)),
         ],
         compiler_params=pltpu.CompilerParams(
-            collective_id=0, has_side_effects=True, vmem_limit_bytes=40 * 1024 * 1024),
-    )(conc, spectra, path_slab.reshape(1, -1), line_offset, profile, beam_absorb, line_absorb)
+            collective_id=0, has_side_effects=True, vmem_limit_bytes=63 * 1024 * 1024),
+    )(*inputs)
 
 
 def solution(mesh):

time: 25.5 us -> 21.3 us (0.84)
  the two profiles are of different devices: /device:TPU:0 before, /device:TPU:5 now
where the time goes in v2:
time: 21.3 us; the launch traced here: 21.2 us
  Pallas kernels  19.3 us (91%)
  local copies, waits for them, and re-layouts  1.88 us (9%)
    pallas_call x1, Pallas kernels, local(): pl.pallas_call(functools.partial(kernel, slabs, views, cells), out_shape=...  19.3 us
    unnamed x1, local copies, waits for them, and re-layouts  1.88 us

profile of v2, /device:TPU:5, one launch (start us, length us, event | category | flops | bytes accessed | tf_op | source)
XLA Modules:
  0.0 21.2 jit_solution(8549494853907732710)
XLA Ops:
  0.0 19.3 %shard_map.73 = f32[8,2,16,512]{3,2,1,0:T(8,128)} custom-call(bf16[8,2,16,2048]{3,2,1,0:T(8,128)(2,1)} %conc_ref.1, bf16[1,64,256]{2,1,0:T(8,128)(2,1)} %refs_0_.1, s32[1,64]{1,0:T(1,128)} %bitcast.1, s32[1,64]{1,0:T(1,128)} %refs_2_.1, f32[8,256]{1,0:T(8,128)} %refs_3_.1, f32[8]{0:T(128)} %refs_4_.1, f32[8,8]{1,0:T(8,128)} %refs_5_.1), custom_call_target="tpu_custom_call" | custom-call | tf_op jit(solution)/shard_map/pallas_call | solution.py:368
  19.3 1.9 %copy.9 = f32[8,2,16,512]{3,2,1,0:T(8,128)} copy(f32[8,2,16,512]{3,2,1,0:T(8,128)} %shard_map.73) | data formatting | bytes 1048576

commit v3 on v2

--- a/solution.py
+++ b/solution.py
@@ -52,7 +52,7 @@
     small_in, out_ref, small_refs, rest = refs[:6], refs[6], refs[7:13], refs[13:]
     spectra_ref, dest_ref, offset_ref, profile_ref, beam_ref, absorb_ref = small_refs
     (own, low, high, low_out, high_out, fwd_hi, fwd_lo, back_hi, back_lo, tri, gram_hi, gram_lo,
-     passing, beams, weights, ray_send, ray_recv, tab, part, column, load_sem, small_sem,
+     passing, beams, weights, ray_send, ray_recv, tab, part, column, stack, result, load_sem, small_sem, out_sem,
      halo_send_sem, halo_recv_sem, ray_send_sem, ray_recv_sem, tab_send_sem, tab_recv_sem,
      part_send_sem, part_recv_sem) = rest
     me, block = lax.axis_index("slab"), lax.axis_index("ang")
@@ -89,16 +89,6 @@
     def _():
         high[...] = jnp.zeros_like(high)
 
-    for s in range(S):
-        loads[s].wait()
-        for i in range(E // 2):
-            first = own[s, 2 * i].astype(f32)
-            second = own[s, 2 * i + 1].astype(f32)
-            low_out[s, i] = jnp.concatenate([first[:H], second[:H]], axis=0).astype(bf16)
-            high_out[s, i] = jnp.concatenate([first[H:], second[H:]], axis=0).astype(bf16)
-
-    pl.semaphore_wait(barrier, slabs - 1 + views - 1)
-
     def halo(s, upward):
         if upward:
             src, dst, target = high_out, low, me + 1
@@ -110,6 +100,15 @@
             device_id={"slab": target, "ang": block}, device_id_type=MESH)
 
     for s in range(S):
+        loads[s].wait()
+        for i in range(E // 2):
+            first = own[s, 2 * i].astype(f32)
+            second = own[s, 2 * i + 1].astype(f32)
+            low_out[s, i] = jnp.concatenate([first[:H], second[:H]], axis=0).astype(bf16)
+            high_out[s, i] = jnp.concatenate([first[H:], second[H:]], axis=0).astype(bf16)
+        if s == 0:
+            pl.semaphore_wait(barrier, slabs - 1 + views - 1)
+
         @pl.when(me < slabs - 1)
         def _():
             halo(s, True).start()
@@ -202,8 +201,23 @@
         wide = dot(dot(g_hot, piece).astype(bf16), spread.astype(bf16))
         ref[...] = jnp.where(g_row == k_row, wide, 0.0).astype(bf16)
 
+    def gather_rays(k, total):
+        ray_copy(k).wait()
+        return total + ray_recv[k]
+
+    def to_view(src, dst, k, send, recv):
+        return pltpu.make_async_remote_copy(
+            src_ref=src, dst_ref=dst, send_sem=send, recv_sem=recv,
+            device_id={"slab": me, "ang": lax.rem(block + k, views)}, device_id_type=MESH)
+
+    def tab_copy(k):
+        return to_view(tab.at[0], tab.at[k], k, tab_send_sem.at[k], tab_recv_sem.at[k])
+
+    def part_copy(s, k):
+        return to_view(part.at[s, 0], part.at[s, k], k, part_send_sem.at[s, k], part_recv_sem.at[s, k])
+
     lane = iota((1, 128), 1)
-    column[...] = jnp.zeros_like(column)
+    column[:, SIDE:, :] = jnp.zeros((S, 2 * OWN - SIDE, 128), f32)
     for s in range(S):
         @pl.when(me > 0)
         def _():
@@ -212,6 +226,11 @@
         @pl.when(me < slabs - 1)
         def _():
             halo(s, False).wait_recv()
+
+        if s == S - 1:
+            tab[0] = lax.fori_loop(1, slabs, gather_rays, mine)
+            for k in range(1, views):
+                tab_copy(k).start()
 
         maps = jnp.concatenate([own[s], low[s], high[s]], axis=0).reshape(2 * OWN, width)
         paths = dot(fwd_hi[...], maps) + dot(fwd_lo[...], maps)
@@ -224,14 +243,14 @@
         beams[s, 1] = jnp.exp(-scale * (total - before - mu))
 
         def put(rows, values, sums):
-            merged = column[rows, :]
+            merged = jnp.zeros((rows.stop - rows.start, 128), f32)
             for odd_side in range(2):
                 for back in range(2):
-                    k = 2 * (2 * back + odd_side) + s
+                    k = 2 * back + odd_side
                     flux = jnp.sum(values[odd_side][back], axis=1, keepdims=True)
                     merged = jnp.where(lane == k, flux, merged)
-                    merged = jnp.where(lane == 8 + k, sums[odd_side], merged)
-            column[rows, :] = merged
+                    merged = jnp.where(lane == views + k, sums[odd_side], merged)
+            column[s, rows, :] = merged
 
         for e in range(E):
             amount = own[s, e].astype(f32)
@@ -251,106 +270,93 @@
                 both.append(jnp.concatenate([total[rows]] * 2, axis=0))
             put(slice(OWN + i * 2 * H, OWN + (i + 1) * 2 * H), values, both)
 
-
-    def gather_rays(k, total):
-        ray_copy(k).wait()
-        return total + ray_recv[k]
-
-    def to_view(ref, k, send, recv):
-        return pltpu.make_async_remote_copy(
-            src_ref=ref.at[0], dst_ref=ref.at[k], send_sem=send.at[k], recv_sem=recv.at[k],
-            device_id={"slab": me, "ang": lax.rem(block + k, views)}, device_id_type=MESH)
-
-    part[0] = jnp.transpose(column[...])[:16]
+        part[s, 0] = jnp.transpose(column[s])[:2 * views]
+        for k in range(1, views):
+            part_copy(s, k).start()
+
     for k in range(1, views):
-        to_view(part, k, part_send_sem, part_recv_sem).start()
-    tab[0] = lax.fori_loop(1, slabs, gather_rays, mine)
-    for k in range(1, views):
-        to_view(tab, k, tab_send_sem, tab_recv_sem).start()
-
-    for k in range(1, views):
-        to_view(tab, k, tab_send_sem, tab_recv_sem).wait()
-
-    row8 = iota((8, 1), 0)
-    sums = jnp.zeros((8, 2 * OWN), f32)
-    counts = jnp.zeros((8, 2 * OWN), f32)
+        tab_copy(k).wait()
+    view_row = iota((views, 1), 0)
+    ahead_rows = view_row < 2
     owner = [lax.rem(block + views - k, views) for k in range(views)]
-    for k in range(views):
-        for s in range(S):
-            here = row8 == 2 * owner[k] + s
+    for s in range(S):
+        sums = jnp.zeros((views, 2 * OWN), f32)
+        counts = jnp.zeros((views, 2 * OWN), f32)
+        for k in range(views):
+            here = view_row == owner[k]
             sums = jnp.where(here, tab[k, s:s + 1, :], sums)
             counts = jnp.where(here, tab[k, S + s:S + s + 1, :], counts)
-
-    for k in range(1, views):
-        to_view(part, k, part_send_sem, part_recv_sem).wait()
-
-    ahead_rows = row8 < 4
-    blocks, scales = [], []
-    for k in range(views):
-        offset = jnp.zeros((8, 2 * OWN), f32)
-        for j in range(views):
-            if j != k:
-                counted = (ahead_rows & (owner[j] < owner[k])) | (~ahead_rows & (owner[j] > owner[k]))
-                offset = offset + jnp.where(counted, part[j, 8:16, :], 0.0)
-        factor = jnp.exp(-scale * offset)
-        scales.append(factor)
-        blocks.append(part[k, 0:8, :] * factor)
-    fluor = (blocks[0] + blocks[1] + blocks[2] + blocks[3]) * scale
-    fluor_hi, fluor_lo = split(fluor)
-    mixed = dot(fluor_hi, gram_hi[...]) + dot(fluor_lo, gram_hi[...]) + dot(fluor_hi, gram_lo[...])
-    pulled = counts * mixed - sums
-    later = jnp.zeros((8, 2 * OWN), f32)
-    for k in range(views):
-        counted = (ahead_rows & (owner[k] >= block)) | (~ahead_rows & (owner[k] < block))
-        later = later + jnp.where(counted, blocks[k], 0.0)
-    pad = jnp.zeros((112, 2 * OWN), f32)
-    stacked = jnp.concatenate([pulled * scales[0], -pulled * later, pad], axis=0)
-    column[...] = jnp.transpose(stacked)
-
-    carry = column[0:R, :]
-    for e in range(1, E):
-        carry = carry + column[e * R:(e + 1) * R, :]
-
-    for s in range(S):
+        for k in range(1, views):
+            part_copy(s, k).wait()
+        blocks, scales = [], []
+        for k in range(views):
+            offset = jnp.zeros((views, 2 * OWN), f32)
+            for j in range(views):
+                if j != k:
+                    counted = (ahead_rows & (owner[j] < owner[k])) | (~ahead_rows & (owner[j] > owner[k]))
+                    offset = offset + jnp.where(counted, part[s, j, views:2 * views, :], 0.0)
+            factor = jnp.exp(-scale * offset)
+            scales.append(factor)
+            blocks.append(part[s, k, 0:views, :] * factor)
+        fluor = (blocks[0] + blocks[1] + blocks[2] + blocks[3]) * scale
+        fluor_hi, fluor_lo = split(fluor)
+        mixed = dot(fluor_hi, gram_hi[...]) + dot(fluor_lo, gram_hi[...]) + dot(fluor_hi, gram_lo[...])
+        pulled = counts * mixed - sums
+        later = jnp.zeros((views, 2 * OWN), f32)
+        for k in range(views):
+            counted = (ahead_rows & (owner[k] >= block)) | (~ahead_rows & (owner[k] < block))
+            later = later + jnp.where(counted, blocks[k], 0.0)
+        stack[0:views, :] = pulled * scales[0]
+        stack[views:2 * views, :] = -pulled * later
+        pad = jnp.zeros((128 - 2 * views, 2 * OWN), f32)
+        column[s] = jnp.transpose(jnp.concatenate([stack[...], pad], axis=0))
+
+        carry = column[s, 0:R, :]
+        for e in range(1, E):
+            carry = carry + column[s, e * R:(e + 1) * R, :]
+
         beam = [beams[s, 0, :R], beams[s, 1, :R]]
         seen = [jnp.zeros((R, width), f32), jnp.zeros((R, width), f32)]
         for e in range(E):
             amount = own[s, e].astype(f32)
-            cols = column[e * R:(e + 1) * R, :]
+            cols = column[s, e * R:(e + 1) * R, :]
             direct = None
             for odd_side in range(2):
                 start = odd_side * SIDE + e * R
                 through = passing[s, start:start + R]
-                ahead_pull = cols[:, 2 * odd_side + s:2 * odd_side + s + 1]
-                back_pull = cols[:, 4 + 2 * odd_side + s:4 + 2 * odd_side + s + 1]
+                ahead_pull = cols[:, odd_side:odd_side + 1]
+                back_pull = cols[:, 2 + odd_side:2 + odd_side + 1]
                 term = through * (ahead_pull * beam[0] + back_pull * beam[1])
                 lit = amount * through
                 seen[0] = seen[0] + lit * ahead_pull
                 seen[1] = seen[1] + lit * back_pull
                 weights[0, start:start + R], weights[1, start:start + R] = split(amount * term)
                 direct = term if direct is None else direct + term
-            out_ref[e, s] = direct
+            result[s, e] = direct
         for i in range(E // 2):
-            cols = column[OWN + i * 2 * H:OWN + (i + 1) * 2 * H, :]
+            cols = column[s, OWN + i * 2 * H:OWN + (i + 1) * 2 * H, :]
             for odd_side, ref in ((0, low), (1, high)):
                 start = odd_side * SIDE + OWN + i * 2 * H
                 rows = slice(R + odd_side * H, R + (odd_side + 1) * H)
                 beam_h = [jnp.concatenate([beams[s, back, rows]] * 2, axis=0) for back in range(2)]
-                ahead_pull = cols[:, 2 * odd_side + s:2 * odd_side + s + 1]
-                back_pull = cols[:, 4 + 2 * odd_side + s:4 + 2 * odd_side + s + 1]
+                ahead_pull = cols[:, odd_side:odd_side + 1]
+                back_pull = cols[:, 2 + odd_side:2 + odd_side + 1]
                 term = passing[s, start:start + 2 * H] * (ahead_pull * beam_h[0] + back_pull * beam_h[1])
                 weights[0, start:start + 2 * H], weights[1, start:start + 2 * H] = split(ref[s, i].astype(f32) * term)
         lines = dot(back_hi[...], weights[0]) + dot(back_lo[...], weights[0]) + dot(back_hi[...], weights[1])
         ahead_sum = beam[0] * seen[0]
         back_sum = beam[1] * seen[1]
         diff_hi, diff_lo = split(ahead_sum - back_sum)
-        chosen = (lane >= 8) & (lane < 16) & (lane % 2 == s)
+        chosen = (lane >= views) & (lane < 2 * views)
         extra = jnp.sum(jnp.where(chosen, carry, 0.0), axis=1, keepdims=True)
         back_beam = scale * (dot(diff_hi, tri[...]) + dot(diff_lo, tri[...]) + ahead_sum + extra)
         for e in range(E):
-            out_ref[e, s] = out_ref[e, s] + beam_ref[e] * back_beam - lines[e * R:(e + 1) * R]
+            result[s, e] = result[s, e] + beam_ref[e] * back_beam - lines[e * R:(e + 1) * R]
+        pltpu.make_async_copy(result.at[s], out_ref.at[:, s], out_sem.at[s]).start()
 
     for s in range(S):
+        pltpu.make_async_copy(result.at[s], out_ref.at[:, s], out_sem.at[s]).wait()
+
         @pl.when(me < slabs - 1)
         def _():
             halo(s, True).wait_send()
@@ -369,7 +375,7 @@
         functools.partial(kernel, slabs, views, cells),
         out_shape=jax.ShapeDtypeStruct((E, S, R, width), f32),
         in_specs=[pl.BlockSpec(memory_space=pltpu.HBM)] * len(inputs),
-        out_specs=pl.BlockSpec(memory_space=pltpu.VMEM),
+        out_specs=pl.BlockSpec(memory_space=pltpu.HBM),
         scratch_shapes=[
             pltpu.SMEM(x.shape, x.dtype) if x is beam_absorb else pltpu.VMEM(x.shape, x.dtype) for x in inputs[1:]
         ] + [
@@ -391,18 +397,21 @@
             pltpu.VMEM((slabs, 8, 2 * OWN), f32),
             pltpu.VMEM((slabs, 8, 2 * OWN), f32),
             pltpu.VMEM((views, 8, 2 * OWN), f32),
-            pltpu.VMEM((views, 16, 2 * OWN), f32),
-            pltpu.VMEM((2 * OWN, 128), f32),
+            pltpu.VMEM((S, views, 2 * views, 2 * OWN), f32),
+            pltpu.VMEM((S, 2 * OWN, 128), f32),
+            pltpu.VMEM((2 * views, 2 * OWN), f32),
+            pltpu.VMEM((S, E, R, width), f32),
             dma((S,)),
             dma((len(inputs) - 1,)),
+            dma((S,)),
             dma((2, S)),
             dma((2, S)),
             dma((slabs,)),
             dma((slabs,)),
             dma((views,)),
             dma((views,)),
-            dma((views,)),
-            dma((views,)),
+            dma((S, views)),
+            dma((S, views)),
         ],
         compiler_params=pltpu.CompilerParams(
             collective_id=0, has_side_effects=True, vmem_limit_bytes=63 * 1024 * 1024),

time: 21.3 us -> 21.1 us (level); the launches traced: 21.2 us -> 20.8 us
  Pallas kernels: 19.3 us -> 18.9 us
    pallas_call x1, Pallas kernels: 19.3 us -> 18.9 us  [local(): pl.pallas_call(functools.partial(kernel, slabs, views, cells), out_shape=...]
where the time goes in v3:
time: 21.1 us; the launch traced here: 20.8 us
  Pallas kernels  18.9 us (90%)
  local copies, waits for them, and re-layouts  1.88 us (9%)
    pallas_call x1, Pallas kernels, local(): pl.pallas_call(functools.partial(kernel, slabs, views, cells), out_shape=...  18.9 us
    unnamed x1, local copies, waits for them, and re-layouts  1.88 us

profile of v3, /device:TPU:5, one launch (start us, length us, event | category | flops | bytes accessed | tf_op | source)
XLA Modules:
  0.0 20.8 jit_solution(4067939542061352307)
XLA Ops:
  0.0 18.9 %shard_map.73 = f32[8,2,16,512]{3,2,1,0:T(8,128)} custom-call(bf16[8,2,16,2048]{3,2,1,0:T(8,128)(2,1)} %conc_ref.1, bf16[1,64,256]{2,1,0:T(8,128)(2,1)} %refs_0_.1, s32[1,64]{1,0:T(1,128)} %bitcast.1, s32[1,64]{1,0:T(1,128)} %refs_2_.1, f32[8,256]{1,0:T(8,128)} %refs_3_.1, f32[8]{0:T(128)} %refs_4_.1, f32[8,8]{1,0:T(8,128)} %refs_5_.1), custom_call_target="tpu_custom_call" | custom-call | tf_op jit(solution)/shard_map/pallas_call | solution.py:374
  18.9 1.9 %copy.9 = f32[8,2,16,512]{3,2,1,0:T(8,128)} copy(f32[8,2,16,512]{3,2,1,0:T(8,128)} %shard_map.73) | data formatting | bytes 1048576

commit v4 on v3

--- a/solution.py
+++ b/solution.py
@@ -52,7 +52,7 @@
     small_in, out_ref, small_refs, rest = refs[:6], refs[6], refs[7:13], refs[13:]
     spectra_ref, dest_ref, offset_ref, profile_ref, beam_ref, absorb_ref = small_refs
     (own, low, high, low_out, high_out, fwd_hi, fwd_lo, back_hi, back_lo, tri, gram_hi, gram_lo,
-     passing, beams, weights, ray_send, ray_recv, tab, part, column, stack, result, load_sem, small_sem, out_sem,
+     passing, beams, weights, ray_send, ray_recv, tab, part, column, stack, load_sem, small_sem,
      halo_send_sem, halo_recv_sem, ray_send_sem, ray_recv_sem, tab_send_sem, tab_recv_sem,
      part_send_sem, part_recv_sem) = rest
     me, block = lax.axis_index("slab"), lax.axis_index("ang")
@@ -332,7 +332,7 @@
                 seen[1] = seen[1] + lit * back_pull
                 weights[0, start:start + R], weights[1, start:start + R] = split(amount * term)
                 direct = term if direct is None else direct + term
-            result[s, e] = direct
+            out_ref[e, s] = direct
         for i in range(E // 2):
             cols = column[s, OWN + i * 2 * H:OWN + (i + 1) * 2 * H, :]
             for odd_side, ref in ((0, low), (1, high)):
@@ -351,11 +351,7 @@
         extra = jnp.sum(jnp.where(chosen, carry, 0.0), axis=1, keepdims=True)
         back_beam = scale * (dot(diff_hi, tri[...]) + dot(diff_lo, tri[...]) + ahead_sum + extra)
         for e in range(E):
-            result[s, e] = result[s, e] + beam_ref[e] * back_beam - lines[e * R:(e + 1) * R]
-        pltpu.make_async_copy(result.at[s], out_ref.at[:, s], out_sem.at[s]).start()
-
-    for s in range(S):
-        pltpu.make_async_copy(result.at[s], out_ref.at[:, s], out_sem.at[s]).wait()
+            out_ref[e, s] = out_ref[e, s] + beam_ref[e] * back_beam - lines[e * R:(e + 1) * R]
 
         @pl.when(me < slabs - 1)
         def _():
@@ -375,7 +371,7 @@
         functools.partial(kernel, slabs, views, cells),
         out_shape=jax.ShapeDtypeStruct((E, S, R, width), f32),
         in_specs=[pl.BlockSpec(memory_space=pltpu.HBM)] * len(inputs),
-        out_specs=pl.BlockSpec(memory_space=pltpu.HBM),
+        out_specs=pl.BlockSpec(memory_space=pltpu.VMEM),
         scratch_shapes=[
             pltpu.SMEM(x.shape, x.dtype) if x is beam_absorb else pltpu.VMEM(x.shape, x.dtype) for x in inputs[1:]
         ] + [
@@ -400,10 +396,8 @@
             pltpu.VMEM((S, views, 2 * views, 2 * OWN), f32),
             pltpu.VMEM((S, 2 * OWN, 128), f32),
             pltpu.VMEM((2 * views, 2 * OWN), f32),
-            pltpu.VMEM((S, E, R, width), f32),
             dma((S,)),
             dma((len(inputs) - 1,)),
-            dma((S,)),
             dma((2, S)),
             dma((2, S)),
             dma((slabs,)),
@@ -414,8 +408,8 @@
             dma((S, views)),
         ],
         compiler_params=pltpu.CompilerParams(
-            collective_id=0, has_side_effects=True, vmem_limit_bytes=63 * 1024 * 1024),
-    )(*inputs)
+            collective_id=0, has_side_effects=True, vmem_limit_bytes=40 * 1024 * 1024),
+    )(*[pltpu.with_memory_space_constraint(x, pltpu.HBM) for x in inputs])
 
 
 def solution(mesh):

time: 21.1 us -> 19.4 us (0.919)
  local copies, waits for them, and re-layouts: 1.88 us -> 0.8 us
  Pallas kernels: 18.9 us -> 18.2 us
    unnamed x1, local copies, waits for them, and re-layouts: 1.88 us -> 0.8 us
    pallas_call x1, Pallas kernels: 18.9 us -> 18.2 us  [local(): pl.pallas_call(functools.partial(kernel, slabs, views, cells), out_shape=...]
where the time goes in v4:
time: 19.4 us; the launch traced here: 19 us
  Pallas kernels  18.2 us (94%)
  local copies, waits for them, and re-layouts  0.8 us (4%)
    pallas_call x1, Pallas kernels, local(): pl.pallas_call(functools.partial(kernel, slabs, views, cells), out_shape=...  18.2 us
    unnamed x1, local copies, waits for them, and re-layouts  0.8 us

profile of v4, /device:TPU:5, one launch (start us, length us, event | category | flops | bytes accessed | tf_op | source)
XLA Modules:
  0.0 19.0 jit_solution(15699399542260028673)
XLA Ops:
  0.0 18.2 %shard_map.73 = f32[8,2,16,512]{3,2,1,0:T(8,128)S(1)} custom-call(bf16[8,2,16,2048]{3,2,1,0:T(8,128)(2,1)} %conc_ref.1, bf16[1,64,256]{2,1,0:T(8,128)(2,1)} %refs_0_.1, s32[1,64]{1,0:T(1,128)} %bitcast.1, s32[1,64]{1,0:T(1,128)} %refs_2_.1, f32[8,256]{1,0:T(8,128)} %refs_3_.1, f32[8]{0:T(128)} %refs_4_.1, f32[8,8]{1,0:T(8,128)} %refs_5_.1), custom_call_target="tpu_custom_call" | custom-call | tf_op jit(solution)/shard_map/pallas_call | solution.py:370
  18.2 0.8 %copy.9 = f32[8,2,16,512]{3,2,1,0:T(8,128)} copy(f32[8,2,16,512]{3,2,1,0:T(8,128)S(1)} %shard_map.73) | data formatting | bytes 1048576

commit v5 on v4

--- a/solution.py
+++ b/solution.py
@@ -65,21 +65,21 @@
             conc_ref.at[:, s, :, pl.ds(pl.multiple_of(block * width, 128), width)], own.at[s], load_sem.at[s])
         copy.start()
         loads.append(copy)
+    barrier = pltpu.get_barrier_semaphore()
+
+    def greet(k, carry):
+        pl.semaphore_signal(barrier, inc=1, device_id={"slab": lax.rem(me + k, slabs), "ang": block}, device_id_type=MESH)
+        return carry
+
+    lax.fori_loop(1, slabs, greet, 0)
+    for k in range(1, views):
+        pl.semaphore_signal(barrier, inc=1, device_id={"slab": me, "ang": lax.rem(block + k, views)}, device_id_type=MESH)
+
     small_loads = []
     for i in range(6):
         copy = pltpu.make_async_copy(small_in[i], small_refs[i], small_sem.at[i])
         copy.start()
         small_loads.append(copy)
-
-    barrier = pltpu.get_barrier_semaphore()
-
-    def greet(k, carry):
-        pl.semaphore_signal(barrier, inc=1, device_id={"slab": lax.rem(me + k, slabs), "ang": block}, device_id_type=MESH)
-        return carry
-
-    lax.fori_loop(1, slabs, greet, 0)
-    for k in range(1, views):
-        pl.semaphore_signal(barrier, inc=1, device_id={"slab": me, "ang": lax.rem(block + k, views)}, device_id_type=MESH)
 
     @pl.when(me == 0)
     def _():
@@ -227,11 +227,6 @@
         def _():
             halo(s, False).wait_recv()
 
-        if s == S - 1:
-            tab[0] = lax.fori_loop(1, slabs, gather_rays, mine)
-            for k in range(1, views):
-                tab_copy(k).start()
-
         maps = jnp.concatenate([own[s], low[s], high[s]], axis=0).reshape(2 * OWN, width)
         paths = dot(fwd_hi[...], maps) + dot(fwd_lo[...], maps)
         passing[s] = jnp.exp(-paths[:LINES])
@@ -241,6 +236,11 @@
         total = jnp.sum(mu, axis=1, keepdims=True)
         beams[s, 0] = jnp.exp(-scale * before)
         beams[s, 1] = jnp.exp(-scale * (total - before - mu))
+
+        if s == S - 1:
+            tab[0] = lax.fori_loop(1, slabs, gather_rays, mine)
+            for k in range(1, views):
+                tab_copy(k).start()
 
         def put(rows, values, sums):
             merged = jnp.zeros((rows.stop - rows.start, 128), f32)

time: 19.4 us -> 19.7 us (1.015); the launches traced: 19 us -> 19.6 us
  Pallas kernels: 18.2 us -> 18.8 us
    pallas_call x1, Pallas kernels: 18.2 us -> 18.8 us  [local(): pl.pallas_call(functools.partial(kernel, slabs, views, cells), out_shape=...]
where the time goes in v5:
time: 19.7 us; the launch traced here: 19.6 us
  Pallas kernels  18.8 us (95%)
  local copies, waits for them, and re-layouts  0.8 us (4%)
    pallas_call x1, Pallas kernels, local(): pl.pallas_call(functools.partial(kernel, slabs, views, cells), out_shape=...  18.8 us
    unnamed x1, local copies, waits for them, and re-layouts  0.8 us

profile of v5, /device:TPU:5, one launch (start us, length us, event | category | flops | bytes accessed | tf_op | source)
XLA Modules:
  0.0 19.6 jit_solution(2955837559758053045)
XLA Ops:
  0.0 18.8 %shard_map.73 = f32[8,2,16,512]{3,2,1,0:T(8,128)S(1)} custom-call(bf16[8,2,16,2048]{3,2,1,0:T(8,128)(2,1)} %conc_ref.1, bf16[1,64,256]{2,1,0:T(8,128)(2,1)} %refs_0_.1, s32[1,64]{1,0:T(1,128)} %bitcast.1, s32[1,64]{1,0:T(1,128)} %refs_2_.1, f32[8,256]{1,0:T(8,128)} %refs_3_.1, f32[8]{0:T(128)} %refs_4_.1, f32[8,8]{1,0:T(8,128)} %refs_5_.1), custom_call_target="tpu_custom_call" | custom-call | tf_op jit(solution)/shard_map/pallas_call | solution.py:370
  18.8 0.8 %copy.9 = f32[8,2,16,512]{3,2,1,0:T(8,128)} copy(f32[8,2,16,512]{3,2,1,0:T(8,128)S(1)} %shard_map.73) | data formatting | bytes 1048576
